TPU v7x, 256 devices: a whole 4x4x8 slice. The times are simulated.
256 devices in a mesh: chan: 32 (over x, z_lo, y), ablk: 8 (over z_hi, core).
Axes of the slice: x: 4, y: 4, z: 8 (z_hi: 4, z_lo: 2; z = z_hi * 2 + z_lo), core: 2. Of those that a mesh axis runs over, the one named last changes fastest.
Arguments:
- voltages: int32 [2, 4096, 32, 512], P(None, ('chan', 'ablk')), may hold values from -7 to 7
- complex_gains: float32 [2, 4096, 32], P(None, ('chan', 'ablk')), may hold values from -4 to 4
Outputs:
- visibilities: float32 [32, 2, 18432, 512], P('chan', None, 'ablk')
All inputs are finite; a program needn't handle non-finite values.
Results may differ from a plain program's by a relative error of at most 0.0034.
Values may be sent and summed in bfloat16 or wider, within the bound.
A program may use at most 64 MiB of HBM per device.

v0:
```python
import jax
import jax.numpy as jnp
from jax import lax
from jax.sharding import PartitionSpec as P


def from_behind(block, axis, distance):
    devices = range(lax.axis_size(axis))
    route = [((i - distance) % len(devices), i) for i in devices]
    return lax.ppermute(block, axis, route)


def block_pair(left_rows, right_rows, norm_factor):
    channel_count = left_rows.shape[0]
    row_count = left_rows.shape[2]
    block_rows = right_rows.shape[2]
    samples = left_rows.shape[3]
    left_flat = left_rows.reshape(channel_count, 2 * row_count, samples)
    right_flat = right_rows.reshape(channel_count, 2 * block_rows, samples)
    products = jnp.einsum("cit,cjt->cij", left_flat, right_flat, preferred_element_type=jnp.float32)
    products = products.reshape(channel_count, 2, row_count, 2, block_rows)
    real_part = products[:, 0, :, 0] + products[:, 1, :, 1]
    imag_part = products[:, 1, :, 0] - products[:, 0, :, 1]
    return jnp.stack((real_part, imag_part), axis=1) * norm_factor


def body(voltages, complex_gains):
    volt_re = voltages[0].astype(jnp.float32)
    volt_im = voltages[1].astype(jnp.float32)
    gain_re = complex_gains[0][:, :, None]
    gain_im = complex_gains[1][:, :, None]
    calibrated = jnp.stack(
        (gain_re * volt_re - gain_im * volt_im, gain_re * volt_im + gain_im * volt_re), axis=0
    ).astype(jnp.bfloat16)
    outgoing = jnp.transpose(calibrated, (2, 0, 1, 3))
    local_block = lax.all_to_all(outgoing, "chan", split_axis=0, concat_axis=2, tiled=True)
    block_rows = local_block.shape[2]
    samples = local_block.shape[3]
    norm_factor = 1.0 / (4.0 * samples)
    groups = lax.axis_size("ablk")
    midway = groups // 2
    position = lax.axis_index("ablk")

    def slot_for(offset, partner):
        if offset < midway:
            return block_pair(local_block, partner, norm_factor)
        upper_half = position >= midway
        left_full = jnp.where(upper_half, partner, local_block)
        right_full = jnp.where(upper_half, local_block, partner)
        begin_row = jnp.where(upper_half, block_rows // 2, 0).astype(jnp.int32)
        left_rows = lax.dynamic_slice_in_dim(left_full, begin_row, block_rows // 2, 2)
        return block_pair(left_rows, right_full, norm_factor)

    pieces = [block_pair(local_block, local_block, norm_factor)]
    for offset in range(1, midway + 1):
        partner = from_behind(local_block, "ablk", -offset)
        pieces.append(slot_for(offset, partner))
    return jnp.concatenate(pieces, axis=2)


def solution(mesh):
    in_specs = (P(None, ("chan", "ablk"), None, None), P(None, ("chan", "ablk"), None))
    out_specs = P("chan", None, "ablk", None)
    return jax.shard_map(body, mesh=mesh, in_specs=in_specs, out_specs=out_specs, check_vma=False)
```

profile of v0, /device:TPU:1, one launch (start us, length us, event | category | flops | bytes accessed | tf_op | source)
XLA Modules:
  0.0 199.4 jit_solution(8622278239212670763)
XLA Ops:
  0.0 0.0 copy-start.1
  0.0 1.8 fusion.26
  1.8 0.0 copy-done.1
  1.8 0.1 copy.5
  1.9 0.1 copy.7
  1.9 1.2 subtract_convert_fusion
  3.1 0.1 maximum_bitcast_fusion
  3.2 24.5 %all_to_all.18 = bf16[32,2,16,512]{3,2,1,0:T(8,128)(2,1)S(1)} all-to-all(bf16[32,2,16,512]{3,2,1,0:T(8,128)(2,1)S(1)} %maximum_bitcast_fusion), channel_id=1, replica_groups=mesh['chan'=32,'ablk'=8] {'chan'}, dimensions={0} | all-to-all | bytes 2097152 | tf_op jit(solution)/shard_map/all_to_all | solution.py:36
  27.7 0.1 copy.9
  27.8 1.9 collective-permute-start
  29.7 5.1 %collective-permute-start.1 = (bf16[1,2,512,512]{3,2,1,0:T(8,128)(2,1)S(1)}, bf16[1,2,512,512]{3,2,1,0:T(8,128)(2,1)S(1)}, u32[]{:S(2)}, u32[]{:S(2)}) collective-permute-start(bf16[1,2,512,512]{3,2,1,0:T(8,128)(2,1)S(1)} %bitcast.73), channel_id=1, source_target_pairs={{2,0},{3,1},{4,2},{5,3},{6,4},{7,5},{0,6},{1,7},{10,8},{11,9},{12,... | collective-permute-start | bytes 3145736 | tf_op jit(solution)/shard_map/ppermute | solution.py:10
  34.9 1.4 collective-permute-start.2
  36.3 2.9 %collective-permute-start.3 = (bf16[1,2,512,512]{3,2,1,0:T(8,128)(2,1)S(1)}, bf16[1,2,512,512]{3,2,1,0:T(8,128)(2,1)S(1)}, u32[]{:S(2)}, u32[]{:S(2)}) collective-permute-start(bf16[1,2,512,512]{3,2,1,0:T(8,128)(2,1)S(1)} %bitcast.75), channel_id=1, source_target_pairs={{4,0},{5,1},{6,2},{7,3},{0,4},{1,5},{2,6},{3,7},{12,8},{13,9},{14,... | collective-permute-start | bytes 3145736 | tf_op jit(solution)/shard_map/ppermute | solution.py:10
  39.2 1.3 convolution_bitcast_fusion.3
  40.5 0.5 fusion.11
  41.0 0.2 fusion
  41.2 66.2 %collective-permute-done = bf16[1,2,512,512]{3,2,1,0:T(8,128)(2,1)S(1)} collective-permute-done((bf16[1,2,512,512]{3,2,1,0:T(8,128)(2,1)S(1)}, bf16[1,2,512,512]{3,2,1,0:T(8,128)(2,1)S(1)}, u32[]{:S(2)}, u32[]{:S(2)}) %collective-permute-start) | collective-permute-done | bytes 1048608 | tf_op jit(solution)/shard_map/ppermute | solution.py:10
  107.4 1.3 convolution_bitcast_fusion.2
  108.7 0.0 collective-permute-done.1
  108.7 1.3 convolution_bitcast_fusion.1
  110.0 0.5 fusion.9
  110.5 0.5 fusion.7
  111.0 80.1 %collective-permute-done.2 = bf16[1,2,512,512]{3,2,1,0:T(8,128)(2,1)S(1)} collective-permute-done((bf16[1,2,512,512]{3,2,1,0:T(8,128)(2,1)S(1)}, bf16[1,2,512,512]{3,2,1,0:T(8,128)(2,1)S(1)}, u32[]{:S(2)}, u32[]{:S(2)}) %collective-permute-start.2) | collective-permute-done | bytes 1048608 | tf_op jit(solution)/shard_map/ppermute | solution.py:10
  191.0 1.3 convolution_bitcast_fusion
  192.3 0.5 fusion.5
  192.8 0.0 collective-permute-done.3
  192.8 0.8 convolution_bitcast_fusion.4
  193.6 0.2 fusion.20
  193.8 0.2 fusion.1
  194.1 0.2 fusion.2
  194.3 0.2 fusion.3
  194.6 0.0 copy-start
  194.6 3.7 %copy-done = f32[1,2,2304,512]{3,2,1,0:T(8,128)} copy-done((f32[1,2,2304,512]{3,2,1,0:T(8,128)}, f32[1,2,2304,512]{3,2,1,0:T(8,128)S(1)}, u32[]{:S(2)}) %copy-start) | copy-done | bytes 9437208
  198.3 1.1 fusion.12
  (1 shorter events, 0.0 us)
Async XLA Ops:
  0.0 1.8 copy-start.1
  27.8 79.6 %collective-permute-start = (bf16[1,2,512,512]{3,2,1,0:T(8,128)(2,1)S(1)}, bf16[1,2,512,512]{3,2,1,0:T(8,128)(2,1)S(1)}, u32[]{:S(2)}, u32[]{:S(2)}) collective-permute-start(bf16[1,2,512,512]{3,2,1,0:T(8,128)(2,1)S(1)} %bitcast.72), channel_id=1, source_target_pairs={{1,0},{2,1},{3,2},{4,3},{5,4},{6,5},{7,6},{0,7},{9,8},{10,9},{11,1... | collective-permute-start | bytes 3145736 | tf_op jit(solution)/shard_map/ppermute | solution.py:10
  29.7 79.0 %collective-permute-start.1 = (bf16[1,2,512,512]{3,2,1,0:T(8,128)(2,1)S(1)}, bf16[1,2,512,512]{3,2,1,0:T(8,128)(2,1)S(1)}, u32[]{:S(2)}, u32[]{:S(2)}) collective-permute-start(bf16[1,2,512,512]{3,2,1,0:T(8,128)(2,1)S(1)} %bitcast.73), channel_id=1, source_target_pairs={{2,0},{3,1},{4,2},{5,3},{6,4},{7,5},{0,6},{1,7},{10,8},{11,9},{12,... | collective-permute-start | bytes 3145736 | tf_op jit(solution)/shard_map/ppermute | solution.py:10
  34.9 156.2 %collective-permute-start.2 = (bf16[1,2,512,512]{3,2,1,0:T(8,128)(2,1)S(1)}, bf16[1,2,512,512]{3,2,1,0:T(8,128)(2,1)S(1)}, u32[]{:S(2)}, u32[]{:S(2)}) collective-permute-start(bf16[1,2,512,512]{3,2,1,0:T(8,128)(2,1)S(1)} %bitcast.74), channel_id=1, source_target_pairs={{3,0},{4,1},{5,2},{6,3},{7,4},{0,5},{1,6},{2,7},{11,8},{12,9},{13,... | collective-permute-start | bytes 3145736 | tf_op jit(solution)/shard_map/ppermute | solution.py:10
  36.3 156.5 %collective-permute-start.3 = (bf16[1,2,512,512]{3,2,1,0:T(8,128)(2,1)S(1)}, bf16[1,2,512,512]{3,2,1,0:T(8,128)(2,1)S(1)}, u32[]{:S(2)}, u32[]{:S(2)}) collective-permute-start(bf16[1,2,512,512]{3,2,1,0:T(8,128)(2,1)S(1)} %bitcast.75), channel_id=1, source_target_pairs={{4,0},{5,1},{6,2},{7,3},{0,4},{1,5},{2,6},{3,7},{12,8},{13,9},{14,... | collective-permute-start | bytes 3145736 | tf_op jit(solution)/shard_map/ppermute | solution.py:10
  194.6 3.7 %copy-start = (f32[1,2,2304,512]{3,2,1,0:T(8,128)}, f32[1,2,2304,512]{3,2,1,0:T(8,128)S(1)}, u32[]{:S(2)}) copy-start(f32[1,2,2304,512]{3,2,1,0:T(8,128)S(1)} %fusion.3) | copy-start | bytes 28311556
where the time goes:
time: 200 us; the launch traced here: 199 us
  waiting for transfers between devices  146 us (73%)
  blocking collectives  24.5 us (12%)
  starting transfers between devices  11.4 us (6%)
  matrix products  5.92 us (3%)
  local copies, waits for them, and re-layouts  5.73 us (3%)
  other arithmetic  5.41 us (3%)
    ppermute x4, waiting for transfers between devices, from_behind(): return lax.ppermute(block, axis, route)  146 us
    all_to_all x1, blocking collectives, body(): lax.all_to_all(outgoing, 'chan', split_axis=0, concat_axis=2, tiled=True)  24.5 us
    ppermute x4, starting transfers between devices, from_behind(): return lax.ppermute(block, axis, route)  11.4 us
    dot_general x5, matrix products, block_pair(): jnp.einsum('cit,cjt->cij', left_flat, right_flat, preferred_element_type=...  5.92 us
  transfers between devices with their start and end apart: 4, of which 2 were waited for; matrix products, arithmetic and copies ran while one was open for 4% of the time, Pallas kernels for 0%

commit v1 on v0

v1 whole, which is shorter than its diff:
```python
import functools

import jax
import jax.numpy as jnp
from jax import lax
from jax.experimental import pallas as pl
from jax.experimental.pallas import tpu as pltpu
from jax.sharding import PartitionSpec as P

MESH = pl.DeviceIdType.MESH

SIDE = 4
PEERS = SIDE * SIDE
GROUPS = 4
ROWS = 16
LANES = 128
PLUS = 5


def coordinates():
    chan, ablk = lax.axis_index("chan"), lax.axis_index("ablk")
    x, parity, y = chan // 8, (chan // 4) % 2, chan % 4
    return x, y, (ablk // 2) * 2 + parity, ablk % 2


def device(x, y, z, core):
    z = (z + 8) % 8
    return x * 8 + (z % 2) * 4 + y, (z // 2) * 2 + core


def peer(x, y, i):
    return (x + i % SIDE) % SIDE, (y + i // SIDE + i % SIDE) % SIDE


def gather_kernel(volt, gain, blocks, cal, other, stash, block_sem, other_sem, stash_sem, twin_sem, send_sem):
    x, y, z, core = coordinates()
    parity = z % 2
    channels = cal.shape[0]
    lane_tiles = cal.shape[3] // LANES
    step = channels * lane_tiles
    home = z + 1 - 2 * parity
    me_c = x * 8 + parity * 4 + y

    barrier = pltpu.get_barrier_semaphore()

    def greet(i, carry):
        px, py = peer(x, y, i)
        pl.semaphore_signal(barrier, inc=1, device_id=device(px, py, z, core), device_id_type=MESH)
        return carry

    lax.fori_loop(1, PEERS, greet, 0)
    for source in (z + 2, z - 2, home, z - 3 + 4 * parity):
        pl.semaphore_signal(barrier, inc=1, device_id=device(x, y, source, core), device_id_type=MESH)
    pl.semaphore_signal(barrier, inc=1, device_id=device(x, y, z, 1 - core), device_id_type=MESH)

    for f in range(channels):
        gain_re = jnp.broadcast_to(gain[0, :, f : f + 1], (ROWS, LANES))
        gain_im = jnp.broadcast_to(gain[1, :, f : f + 1], (ROWS, LANES))
        for t in range(lane_tiles):
            start = (f // 8 * lane_tiles + t) * 8 + f % 8
            volt_re = volt[pl.ds(start, ROWS, stride=step), :].astype(jnp.float32)
            volt_im = volt[pl.ds(ROWS * step + start, ROWS, stride=step), :].astype(jnp.float32)
            cal[f, 0, :, t * LANES : (t + 1) * LANES] = (gain_re * volt_re - gain_im * volt_im).astype(jnp.bfloat16)
            cal[f, 1, :, t * LANES : (t + 1) * LANES] = (gain_re * volt_im + gain_im * volt_re).astype(jnp.bfloat16)

    pl.semaphore_wait(barrier, PEERS + 4)

    def send(src, dst, kind, sem, to):
        pltpu.make_async_remote_copy(
            src_ref=src, dst_ref=dst, send_sem=send_sem.at[kind], recv_sem=sem, device_id=to, device_id_type=MESH
        ).start()

    def arrived(ref, sem):
        pltpu.make_async_copy(ref, ref, sem).wait()

    def place(i, p):
        px, py = peer(x, y, i)
        return px * 8 + p * 4 + py

    def channel_of(px, py, p):
        return px * 8 + p * 4 + py

    pltpu.make_async_copy(cal.at[me_c], blocks.at[0, :, me_c], block_sem.at[0, 0]).start()
    pltpu.make_async_copy(cal.at[channel_of(x, y, 1 - parity)], other.at[:, 0], other_sem.at[0]).start()

    def scatter(i, carry):
        px, py = (x + SIDE - i % SIDE) % SIDE, (y + 2 * SIDE - i // SIDE - i % SIDE) % SIDE
        to = device(px, py, z, core)
        send(cal.at[channel_of(px, py, parity)], blocks.at[0, :, me_c], 0, block_sem.at[0, i], to)
        send(cal.at[channel_of(px, py, 1 - parity)], other.at[:, i], 1, other_sem.at[i], to)
        return carry

    lax.fori_loop(1, PEERS, scatter, 0)

    def share(slot, c):
        def go():
            send(
                blocks.at[2 * slot, :, c],
                blocks.at[2 * (slot - 1 + core) + 1, :, c],
                2,
                twin_sem.at[slot - 1 + core],
                device(x, y, z, 1 - core),
            )

        if isinstance(slot, int) and slot == 1:
            go()
        else:
            pl.when((slot == 1) | (slot == 2 - 2 * core))(go)

    up, down = device(x, y, z + 2, core), device(x, y, z - 2, core)

    def direct(i, carry):
        c = place(i, parity)
        arrived(blocks.at[0, :, c], block_sem.at[0, i])

        @pl.when(i < PLUS)
        def _():
            send(blocks.at[0, :, c], stash.at[:, i], 3, stash_sem.at[i], up)

        @pl.when(i >= PLUS)
        def _():
            send(blocks.at[0, :, c], blocks.at[2, :, c], 4, block_sem.at[1, i], down)

        share(0, c)
        arrived(other.at[:, i], other_sem.at[i])
        send(other.at[:, i], blocks.at[0, :, c], 5, block_sem.at[0, PEERS + i], device(x, y, home, core))
        send(
            other.at[:, i],
            blocks.at[2 + 2 * parity, :, c],
            6,
            block_sem.at[1 + parity, PEERS + i],
            device(x, y, z - 1 + 4 * parity, core),
        )
        return carry

    lax.fori_loop(0, PEERS, direct, 0)

    def lift(i, carry):
        arrived(stash.at[:, i], stash_sem.at[i])
        send(stash.at[:, i], blocks.at[4, :, place(i, parity)], 7, block_sem.at[2, i], up)
        return carry

    lax.fori_loop(0, PLUS, lift, 0)

    def relay(i, carry):
        mine, theirs = place(i, parity), place(i, 1 - parity)
        arrived(blocks.at[0, :, theirs], block_sem.at[0, PEERS + i])
        share(0, theirs)
        first = 2 - parity
        arrived(blocks.at[2 * first, :, theirs], block_sem.at[first, PEERS + i])
        send(
            blocks.at[2 * first, :, theirs],
            blocks.at[2 * (1 + parity), :, theirs],
            8,
            block_sem.at[1 + parity, PEERS + i],
            device(x, y, z + 2 - 4 * parity, core),
        )
        share(first, theirs)

        @pl.when(i < PLUS)
        def _():
            arrived(blocks.at[4, :, mine], block_sem.at[2, i])
            send(blocks.at[4, :, mine], blocks.at[2, :, mine], 9, block_sem.at[1, i], up)
            share(2, mine)

        @pl.when(i >= PLUS)
        def _():
            arrived(blocks.at[2, :, mine], block_sem.at[1, i])
            send(blocks.at[2, :, mine], blocks.at[4, :, mine], 10, block_sem.at[2, i], down)
            share(1, mine)

        return carry

    lax.fori_loop(0, PEERS, relay, 0)

    def last(i, carry):
        mine, theirs = place(i, parity), place(i, 1 - parity)
        second = 1 + parity
        arrived(blocks.at[2 * second, :, theirs], block_sem.at[second, PEERS + i])
        share(second, theirs)

        @pl.when(i < PLUS)
        def _():
            arrived(blocks.at[2, :, mine], block_sem.at[1, i])
            share(1, mine)

        @pl.when(i >= PLUS)
        def _():
            arrived(blocks.at[4, :, mine], block_sem.at[2, i])
            share(2, mine)

        return carry

    lax.fori_loop(0, PEERS, last, 0)

    def sent(kind, count, slot=0):
        ref = blocks.at[slot, :, pl.ds(0, count)]
        pltpu.make_async_copy(ref, ref, send_sem.at[kind]).wait()

    for kind, count in enumerate((15, 15, 64, PLUS, 11, 16, 16, PLUS, 16, PLUS, 11)):
        if kind != 2:
            sent(kind, count)
    pair = blocks.at[pl.ds(0, 2)]
    pltpu.make_async_copy(pair, pair, send_sem.at[2]).wait()
    arrived(blocks.at[1], twin_sem.at[0])
    arrived(blocks.at[3], twin_sem.at[1])


def pair_kernel(left_ref, right_ref, out_ref, *, scale):
    left_re, left_im = left_ref[0, 0], left_ref[0, 1]
    right_re, right_im = right_ref[0, 0], right_ref[0, 1]

    def dot(a, b):
        return lax.dot_general(a, b, (((1,), (1,)), ((), ())), preferred_element_type=jnp.float32)

    out_ref[0] = (dot(left_re, right_re) + dot(left_im, right_im)) * scale
    out_ref[1] = (dot(left_im, right_re) - dot(left_re, right_im)) * scale


def body(voltages, complex_gains):
    parts, rows, channels, samples = voltages.shape
    tiles = voltages.reshape(parts, rows, channels // 8, 8, samples // LANES, LANES).transpose(0, 1, 2, 4, 3, 5)
    blocks = pl.pallas_call(
        gather_kernel,
        out_shape=jax.ShapeDtypeStruct((5, parts, 32, rows, samples), jnp.bfloat16),
        in_specs=[pl.BlockSpec(memory_space=pltpu.VMEM)] * 2,
        out_specs=pl.BlockSpec(memory_space=pltpu.VMEM),
        scratch_shapes=[
            pltpu.VMEM((channels, parts, rows, samples), jnp.bfloat16),
            pltpu.VMEM((parts, PEERS, rows, samples), jnp.bfloat16),
            pltpu.VMEM((parts, PLUS, rows, samples), jnp.bfloat16),
            pltpu.SemaphoreType.DMA((3, 2 * PEERS)),
            pltpu.SemaphoreType.DMA((PEERS,)),
            pltpu.SemaphoreType.DMA((PLUS,)),
            pltpu.SemaphoreType.DMA((2,)),
            pltpu.SemaphoreType.DMA((11,)),
        ],
        compiler_params=pltpu.CompilerParams(
            collective_id=0, has_side_effects=True, vmem_limit_bytes=40 * 1024 * 1024
        ),
        name="gather",
    )(tiles.reshape(-1, LANES), complex_gains)

    size = 32 * rows
    half = size // 2
    blocks = blocks.reshape(5, parts, size, samples)
    steps = 9
    upper = lax.axis_index("ablk") >= 4

    def left_index(j, flag):
        return (jnp.where((j == 8) & (flag[0] == 1), 4, 0), 0, jnp.where(j == 8, flag[0], j % 2), 0)

    def right_index(j, flag):
        return (jnp.where((j == 8) & (flag[0] == 1), 0, j // 2), 0, 0, 0)

    out = pl.pallas_call(
        functools.partial(pair_kernel_flagged, scale=1.0 / (4.0 * samples)),
        out_shape=jax.ShapeDtypeStruct((parts, steps * half, size), jnp.float32),
        grid_spec=pltpu.PrefetchScalarGridSpec(
            num_scalar_prefetch=1,
            grid=(steps,),
            in_specs=[
                pl.BlockSpec((1, parts, half, samples), left_index),
                pl.BlockSpec((1, parts, size, samples), right_index),
            ],
            out_specs=pl.BlockSpec((parts, half, size), lambda j, flag: (0, j, 0)),
        ),
        compiler_params=pltpu.CompilerParams(vmem_limit_bytes=40 * 1024 * 1024),
        name="pairs",
    )(upper.astype(jnp.int32)[None], blocks, blocks)
    return out[None]


def pair_kernel_flagged(flag, left_ref, right_ref, out_ref, *, scale):
    del flag
    pair_kernel(left_ref, right_ref, out_ref, scale=scale)


def solution(mesh):
    in_specs = (P(None, ("chan", "ablk"), None, None), P(None, ("chan", "ablk"), None))
    out_specs = P("chan", None, "ablk", None)
    return jax.shard_map(body, mesh=mesh, in_specs=in_specs, out_specs=out_specs, check_vma=False)
```

time: 200 us -> 85.8 us (0.43)
  the two profiles are of different devices: /device:TPU:1 before, /device:TPU:105 now
where the time goes in v1:
time: 85.8 us; the launch traced here: 85.7 us
  Pallas kernels  83.3 us (97%)
  local copies, waits for them, and re-layouts  2.31 us (3%)
    pallas_call x1, Pallas kernels, body(): pl.pallas_call(gather_kernel, out_shape=jax.ShapeDtypeStruct((5, parts, 3...  74.5 us
    pallas_call x1, Pallas kernels, body(): pl.pallas_call(functools.partial(pair_kernel_flagged, scale=1.0 / (4.0 *...  8.89 us
    unnamed x4, local copies, waits for them, and re-layouts  2.31 us

profile of v1, /device:TPU:105, one launch (start us, length us, event | category | flops | bytes accessed | tf_op | source)
XLA Modules:
  0.0 85.7 jit_solution(5306341636785016043)
XLA Ops:
  0.0 0.0 copy-start
  0.0 1.6 %copy-done = s32[2,16,32,512]{3,2,1,0:T(8,128)S(1)} copy-done((s32[2,16,32,512]{3,2,1,0:T(8,128)S(1)}, s32[2,16,32,512]{3,2,1,0:T(8,128)}, u32[]{:S(2)}) %copy-start) | copy-done | bytes 2097176
  1.6 0.0 copy-start.1
  1.6 0.7 copy-done.1
  2.3 74.5 %gather.1 = bf16[5,2,32,16,512]{4,3,2,1,0:T(8,128)(2,1)S(1)} custom-call(s32[4096,128]{1,0:T(8,128)S(1)} %bitcast.10, f32[2,16,32]{2,1,0:T(8,128)S(1)} %copy-done.1), custom_call_target="tpu_custom_call" | custom-call | tf_op jit(solution)/shard_map/gather/pallas_call | solution.py:223
  76.8 8.9 %pairs.1 = f32[2,2304,512]{2,1,0:T(8,128)} custom-call(s32[1]{0:T(128)} %bitcast.flag, bf16[5,2,512,512]{3,2,1,0:T(8,128)(2,1)S(1)} %bitcast.8, bf16[5,2,512,512]{3,2,1,0:T(8,128)(2,1)S(1)} %bitcast.9), custom_call_target="tpu_custom_call" | custom-call | tf_op jit(solution)/shard_map/pairs/pallas_call | solution.py:256
Async XLA Ops:
  0.0 1.6 %copy-start = (s32[2,16,32,512]{3,2,1,0:T(8,128)S(1)}, s32[2,16,32,512]{3,2,1,0:T(8,128)}, u32[]{:S(2)}) copy-start(s32[2,16,32,512]{3,2,1,0:T(8,128)} %param.2) | copy-start | bytes 6291460
  1.6 0.7 copy-start.1

commit v2 on v1

v2 whole, which is shorter than its diff:
```python
import functools

import jax
import jax.numpy as jnp
from jax import lax
from jax.experimental import pallas as pl
from jax.experimental.pallas import tpu as pltpu
from jax.sharding import PartitionSpec as P

MESH = pl.DeviceIdType.MESH

SIDE = 4
PEERS = SIDE * SIDE
ROWS = 16
LANES = 128
OCTET = 8
PLUS = 5
DELAY = 8
EARLY = 4
LIFT = 8


def coordinates():
    chan, ablk = lax.axis_index("chan"), lax.axis_index("ablk")
    return chan // 8, chan % 4, (ablk // 2) * 2 + (chan // 4) % 2, ablk % 2


def device(x, y, z, core):
    z = (z + 8) % 8
    return x * 8 + (z % 2) * 4 + y, (z // 2) * 2 + core


def gather_kernel(
    volt, gain_hbm, blocks, raw, gain, cal, other, stash,
    raw_sem, gain_sem, block_sem, other_sem, stash_sem, twin_sem, send_sem,
):
    x, y, z, core = coordinates()
    parity = z % 2
    home = z + 1 - 2 * parity
    lane_tiles = cal.shape[3] // LANES
    step, pitch = OCTET * lane_tiles, raw.shape[2]
    me_c = x * 8 + parity * 4 + y

    gain_copy = pltpu.make_async_copy(gain_hbm, gain, gain_sem)
    gain_copy.start()
    raw_copies = []
    for j in range(SIDE):
        target = (x + SIDE - j) % SIDE
        raw_copies.append(pltpu.make_async_copy(volt.at[:, target], raw.at[j, :, pl.ds(0, step)], raw_sem.at[j]))
        raw_copies[-1].start()

    barrier = pltpu.get_barrier_semaphore()

    def greet(i, carry):
        to = device((x + i // SIDE) % SIDE, (y + i % SIDE) % SIDE, z, core)
        pl.semaphore_signal(barrier, inc=1, device_id=to, device_id_type=MESH)
        return carry

    lax.fori_loop(1, PEERS, greet, 0)
    for source in (z + 2, z - 2, home, z - 3 + 4 * parity):
        pl.semaphore_signal(barrier, inc=1, device_id=device(x, y, source, core), device_id_type=MESH)
    pl.semaphore_signal(barrier, inc=1, device_id=device(x, y, z, 1 - core), device_id_type=MESH)

    def send(src, dst, kind, sem, to):
        pltpu.make_async_remote_copy(
            src_ref=src, dst_ref=dst, send_sem=send_sem.at[kind], recv_sem=sem, device_id=to, device_id_type=MESH
        ).start()

    def arrived(ref, sem):
        pltpu.make_async_copy(ref, ref, sem).wait()

    def place(i, p):
        return (x + i // SIDE) % SIDE * 8 + p * 4 + (y + i % SIDE) % SIDE

    def share(slot, c):
        def go():
            to = slot - 1 + core
            send(blocks.at[2 * slot, :, c], blocks.at[2 * to + 1, :, c], 2, twin_sem.at[to], device(x, y, z, 1 - core))

        if isinstance(slot, int) and slot == 1:
            go()
        else:
            pl.when((slot == 1) | (slot == 2 - 2 * core))(go)

    up, down = device(x, y, z + 2, core), device(x, y, z - 2, core)

    def direct(i, carry):
        c = place(i, parity)
        arrived(blocks.at[0, :, c], block_sem.at[0, i])

        @pl.when(i < PLUS)
        def _():
            send(blocks.at[0, :, c], stash.at[:, i], 3, stash_sem.at[i], up)

        @pl.when(i >= PLUS)
        def _():
            send(blocks.at[0, :, c], blocks.at[2, :, c], 4, block_sem.at[1, i], down)

        arrived(other.at[:, i], other_sem.at[i])
        send(
            other.at[:, i],
            blocks.at[2 + 2 * parity, :, c],
            6,
            block_sem.at[1 + parity, PEERS + i],
            device(x, y, z - 1 + 4 * parity, core),
        )
        send(other.at[:, i], blocks.at[0, :, c], 5, block_sem.at[0, PEERS + i], device(x, y, home, core))
        share(0, c)

        @pl.when((i >= LIFT) & (i < LIFT + PLUS))
        def _():
            k = i - LIFT
            arrived(stash.at[:, k], stash_sem.at[k])
            send(stash.at[:, k], blocks.at[4, :, place(k, parity)], 7, block_sem.at[2, k], up)

        return carry

    gain_copy.wait()
    for j in range(SIDE):
        target = (x + SIDE - j) % SIDE
        raw_copies[j].wait()
        octet = raw.at[j].reshape(2 * ROWS * pitch, LANES)
        gain_re, gain_im = gain[0, :, :OCTET], gain[1, :, :OCTET]
        for o in range(1, SIDE):
            gain_re = jnp.where(target == o, gain[0, :, o * OCTET : (o + 1) * OCTET], gain_re)
            gain_im = jnp.where(target == o, gain[1, :, o * OCTET : (o + 1) * OCTET], gain_im)
        for s in range(OCTET):
            g_re = jnp.broadcast_to(gain_re[:, s : s + 1], (ROWS, LANES))
            g_im = jnp.broadcast_to(gain_im[:, s : s + 1], (ROWS, LANES))
            f = target * OCTET + s
            for t in range(lane_tiles):
                start = t * OCTET + s
                v_re = octet[pl.ds(start, ROWS, stride=pitch), :].astype(jnp.float32)
                v_im = octet[pl.ds(ROWS * pitch + start, ROWS, stride=pitch), :].astype(jnp.float32)
                cal[f, 0, :, t * LANES : (t + 1) * LANES] = (g_re * v_re - g_im * v_im).astype(jnp.bfloat16)
                cal[f, 1, :, t * LANES : (t + 1) * LANES] = (g_re * v_im + g_im * v_re).astype(jnp.bfloat16)

        if j == 0:
            pl.semaphore_wait(barrier, PEERS + 4)
            pltpu.make_async_copy(cal.at[me_c], blocks.at[0, :, me_c], block_sem.at[0, 0]).start()
            pltpu.make_async_copy(cal.at[x * 8 + (1 - parity) * 4 + y], other.at[:, 0], other_sem.at[0]).start()

        def scatter(k, carry, j=j, target=target):
            row = (y + SIDE - k) % SIDE
            to = device(target, row, z, core)
            i = j * SIDE + k
            send(cal.at[target * 8 + parity * 4 + row], blocks.at[0, :, me_c], 0, block_sem.at[0, i], to)
            send(cal.at[target * 8 + (1 - parity) * 4 + row], other.at[:, i], 1, other_sem.at[i], to)
            return carry

        lax.fori_loop(1 if j == 0 else 0, SIDE, scatter, 0)
        if j < EARLY:
            direct(j, 0)

    first, second = 2 - parity, 1 + parity

    def relay(i, carry):
        mine, theirs = place(i, parity), place(i, 1 - parity)
        arrived(blocks.at[2 * first, :, theirs], block_sem.at[first, PEERS + i])
        send(
            blocks.at[2 * first, :, theirs],
            blocks.at[2 * second, :, theirs],
            8,
            block_sem.at[second, PEERS + i],
            device(x, y, z + 2 - 4 * parity, core),
        )
        share(first, theirs)

        @pl.when(i >= PLUS)
        def _():
            arrived(blocks.at[2, :, mine], block_sem.at[1, i])
            send(blocks.at[2, :, mine], blocks.at[4, :, mine], 10, block_sem.at[2, i], down)
            share(1, mine)

        @pl.when((i >= LIFT) & (i < LIFT + PLUS))
        def _():
            k = i - LIFT
            lifted = place(k, parity)
            arrived(blocks.at[4, :, lifted], block_sem.at[2, k])
            send(blocks.at[4, :, lifted], blocks.at[2, :, lifted], 9, block_sem.at[1, k], up)
            share(2, lifted)

        return carry

    def both(i, carry):
        direct(i, 0)

        @pl.when(i >= DELAY)
        def _():
            relay(i - DELAY, 0)

        return carry

    lax.fori_loop(EARLY, PEERS, both, 0)

    lax.fori_loop(PEERS - DELAY, PEERS, relay, 0)

    def last(i, carry):
        mine, theirs = place(i, parity), place(i, 1 - parity)
        arrived(blocks.at[0, :, theirs], block_sem.at[0, PEERS + i])
        share(0, theirs)
        arrived(blocks.at[2 * second, :, theirs], block_sem.at[second, PEERS + i])
        share(second, theirs)

        @pl.when(i < PLUS)
        def _():
            arrived(blocks.at[2, :, mine], block_sem.at[1, i])
            share(1, mine)

        @pl.when(i >= PLUS)
        def _():
            arrived(blocks.at[4, :, mine], block_sem.at[2, i])
            share(2, mine)

        return carry

    lax.fori_loop(0, PEERS, last, 0)

    def sent(kind, count):
        ref = blocks.at[0, :, pl.ds(0, count)]
        pltpu.make_async_copy(ref, ref, send_sem.at[kind]).wait()

    rest = PEERS - PLUS
    for kind, count in ((0, 15), (1, 15), (3, PLUS), (4, rest), (5, 16), (6, 16), (7, PLUS), (8, 16), (9, PLUS), (10, rest)):
        sent(kind, count)
    pair = blocks.at[pl.ds(0, 2)]
    pltpu.make_async_copy(pair, pair, send_sem.at[2]).wait()
    arrived(blocks.at[1], twin_sem.at[0])
    arrived(blocks.at[3], twin_sem.at[1])


def product(left, right):
    rows = jnp.concatenate(
        (jnp.concatenate((left[0], left[1]), axis=1), jnp.concatenate((left[1], -left[0]), axis=1)), axis=0
    )
    columns = jnp.concatenate((right[0], right[1]), axis=1)
    return lax.dot_general(rows, columns, (((1,), (1,)), ((), ())), preferred_element_type=jnp.float32)


def pairs_kernel(blocks, out, made, sem, *, scale):
    upper = (lax.axis_index("ablk") >= 4).astype(jnp.int32)
    steps, parts, half, size = made.shape

    def copy(j):
        return pltpu.make_async_copy(made.at[j], out.at[:, pl.ds(j * half, half)], sem.at[j])

    def make(j):
        if j < steps - 1:
            left, right = blocks[0, :, j % 2 * half : (j % 2 + 1) * half, :], blocks[j // 2]
        else:
            left = blocks[4 * upper, :, pl.ds(pl.multiple_of(upper * half, half), half), :]
            right = blocks[4 - 4 * upper]
        made[j] = (product(left, right) * scale).reshape(parts, half, size)
        copy(j).start()

    for j in range(steps):
        make(j)

    for j in range(steps):
        copy(j).wait()


def body(voltages, complex_gains):
    parts, rows, channels, samples = voltages.shape
    lane_tiles = samples // LANES
    octets = channels // OCTET
    tiles = voltages.reshape(parts, rows, octets, OCTET, lane_tiles, LANES).transpose(0, 1, 2, 4, 3, 5)
    tiles = tiles.reshape(parts * rows, octets, lane_tiles * OCTET, LANES)
    blocks = pl.pallas_call(
        gather_kernel,
        out_shape=pltpu.VMEM((5, parts, 32, rows, samples), jnp.bfloat16),
        in_specs=[pl.BlockSpec(memory_space=pltpu.HBM)] * 2,
        out_specs=pl.BlockSpec(memory_space=pltpu.VMEM),
        scratch_shapes=[
            pltpu.VMEM((octets, parts * rows, lane_tiles * OCTET + 8, LANES), jnp.int32),
            pltpu.VMEM((parts, rows, channels), jnp.float32),
            pltpu.VMEM((channels, parts, rows, samples), jnp.bfloat16),
            pltpu.VMEM((parts, PEERS, rows, samples), jnp.bfloat16),
            pltpu.VMEM((parts, PLUS, rows, samples), jnp.bfloat16),
            pltpu.SemaphoreType.DMA((SIDE,)),
            pltpu.SemaphoreType.DMA,
            pltpu.SemaphoreType.DMA((3, 2 * PEERS)),
            pltpu.SemaphoreType.DMA((PEERS,)),
            pltpu.SemaphoreType.DMA((PLUS,)),
            pltpu.SemaphoreType.DMA((2,)),
            pltpu.SemaphoreType.DMA((11,)),
        ],
        compiler_params=pltpu.CompilerParams(
            collective_id=0, has_side_effects=True, vmem_limit_bytes=40 * 1024 * 1024
        ),
        name="gather",
    )(*(pltpu.with_memory_space_constraint(a, pltpu.HBM) for a in (tiles, complex_gains)))

    size = 32 * rows
    half = size // 2
    steps = 9
    out = pl.pallas_call(
        functools.partial(pairs_kernel, scale=1.0 / (4.0 * samples)),
        out_shape=jax.ShapeDtypeStruct((parts, steps * half, size), jnp.float32),
        in_specs=[pl.BlockSpec(memory_space=pltpu.VMEM)],
        out_specs=pl.BlockSpec(memory_space=pl.ANY),
        scratch_shapes=[
            pltpu.VMEM((steps, parts, half, size), jnp.float32),
            pltpu.SemaphoreType.DMA((steps,)),
        ],
        compiler_params=pltpu.CompilerParams(vmem_limit_bytes=40 * 1024 * 1024),
        name="pairs",
    )(blocks.reshape(5, parts, size, samples))
    return out[None]


def solution(mesh):
    in_specs = (P(None, ("chan", "ablk"), None, None), P(None, ("chan", "ablk"), None))
    out_specs = P("chan", None, "ablk", None)
    return jax.shard_map(body, mesh=mesh, in_specs=in_specs, out_specs=out_specs, check_vma=False)
```

time: 85.8 us -> 77.1 us (0.90)
  the two profiles are of different devices: /device:TPU:105 before, /device:TPU:1 now
where the time goes in v2:
time: 77.1 us; the launch traced here: 77 us
  Pallas kernels  77 us (100%)
    pallas_call x1, Pallas kernels, body(): pl.pallas_call(gather_kernel, out_shape=pltpu.VMEM((5, parts, 32, rows, s...  70.8 us
    pallas_call x1, Pallas kernels, body(): pl.pallas_call(functools.partial(pairs_kernel, scale=1.0 / (4.0 * samples...  6.13 us

profile of v2, /device:TPU:1, one launch (start us, length us, event | category | flops | bytes accessed | tf_op | source)
XLA Modules:
  0.0 77.0 jit_solution(6721615702874805050)
XLA Ops:
  0.0 70.8 %gather.1 = bf16[5,2,32,16,512]{4,3,2,1,0:T(8,128)(2,1)S(1)} custom-call(s32[32,4,32,128]{3,2,1,0:T(8,128)} %bitcast.8, f32[2,16,32]{2,1,0:T(8,128)} %gain_hbm.1), custom_call_target="tpu_custom_call" | custom-call | tf_op jit(solution)/shard_map/gather/pallas_call | solution.py:269
  70.8 6.1 %pairs.1 = f32[2,2304,512]{2,1,0:T(8,128)} custom-call(bf16[5,2,512,512]{3,2,1,0:T(8,128)(2,1)S(1)} %bitcast.7), custom_call_target="tpu_custom_call" | custom-call | tf_op jit(solution)/shard_map/pairs/pallas_call | solution.py:297

commit v3 on v0

v3 whole, which is shorter than its diff:
```python
import functools

import jax
import jax.numpy as jnp
from jax import lax
from jax.experimental import pallas as pl
from jax.experimental.pallas import tpu as pltpu
from jax.sharding import PartitionSpec as P

MESH = pl.DeviceIdType.MESH

SIDE = 4
PEERS = SIDE * SIDE
ROWS = 16
LANES = 128
OCTET = 8
GROUPS = 4
UPS = 4, 4, 6, 4
DELAY = 8
EARLY = 4


def wrap(i):
    return lax.rem(i + SIDE, SIDE)


def gather_kernel(
    volt, gain_hbm, blocks, diagonal, begun, raw, gain, cal, other, stash,
    raw_sem, gain_sem, block_sem, other_sem, stash_sem, twin_sem, send_sem,
):
    chan, ablk = lax.axis_index("chan"), lax.axis_index("ablk")
    x, y, parity = chan // 8, lax.rem(chan, 4), lax.rem(chan // 4, 2)
    group, core = ablk // 2, lax.rem(ablk, 2)
    size = blocks.shape[2] * ROWS
    scale = 1.0 / (4.0 * cal.shape[3])
    lane_tiles = cal.shape[3] // LANES
    step, pitch = OCTET * lane_tiles, raw.shape[2]
    flipped = 1 - parity
    xs = [8 * wrap(x + o) for o in range(SIDE)]
    ys = [wrap(y + o) for o in range(SIDE)]
    mine, theirs = 4 * parity, 4 * flipped
    me_c, flip_c = chan, xs[0] + ys[0] + theirs

    def place(i, p):
        return xs[i // SIDE] + ys[i % SIDE] + p

    ranks = [4 * wrap(x + o) for o in range(SIDE)]

    def rank(i):
        return ranks[i // SIDE] + ys[i % SIDE]

    def ups(distance):
        g = wrap(group + distance)
        count = jnp.where(g == 0, UPS[0], UPS[1])
        for k in range(2, GROUPS):
            count = jnp.where(g == k, UPS[k], count)
        return count

    def spared(distance):
        return core * jnp.where(wrap(group + distance) < 2, PEERS // 2, 0)

    up_own, up_below, up_next, up_after = ups(0), ups(-1), ups(1), ups(2)
    spared_next, spared_after = spared(1), spared(2)

    def rises(i, count):
        return i < count

    def along(distance, flip=False):
        return (flip_c if flip else chan), 2 * wrap(group + distance) + core

    twin_device = (chan, 2 * group + 1 - core)
    up, down = along(1), along(-1)
    home = flip_c, ablk
    far, onward, far_source = along(3 * parity - 1, True), along(1 - 2 * parity), along(3 * parity - 2, True)

    gain_copy = pltpu.make_async_copy(gain_hbm, gain, gain_sem)
    gain_copy.start()
    raw_copies = []
    for j in range(SIDE):
        target = wrap(x - j)
        raw_copies.append(pltpu.make_async_copy(volt.at[:, target], raw.at[j, :, pl.ds(0, step)], raw_sem.at[j]))
        raw_copies[-1].start()

    barrier = pltpu.get_barrier_semaphore()

    for to in [(place(i, mine), ablk) for i in range(1, PEERS)] + [up, down, home, far_source, twin_device]:
        pl.semaphore_signal(barrier, inc=1, device_id=to, device_id_type=MESH)

    def send(src, dst, kind, sem, to):
        pltpu.make_async_remote_copy(
            src_ref=src, dst_ref=dst, send_sem=send_sem.at[kind], recv_sem=sem, device_id=to, device_id_type=MESH
        ).start()

    def arrived(ref, sem):
        pltpu.make_async_copy(ref, ref, sem).wait()

    def share(slot, c, i):
        def go():
            to = slot - 1 + core
            sem = twin_sem.at[to, i // (PEERS // 2)]
            send(blocks.at[2 * slot, :, c], blocks.at[2 * to + 1, :, c], 2, sem, twin_device)

        if isinstance(slot, int) and slot == 1:
            go()
        else:
            pl.when((slot == 1) | (slot == 2 - 2 * core))(go)

    def direct(i):
        c = place(i, mine)
        own, across = blocks.at[0, :, c], other.at[:, i]
        if i == 0:
            own, across = cal.at[me_c], cal.at[flip_c]
        else:
            arrived(own, block_sem.at[0, i])
        rising = rises(i, up_own)

        @pl.when(rising)
        def _():
            send(own, stash.at[:, i], 3, stash_sem.at[i], up)

        @pl.when(jnp.logical_not(rising))
        def _():
            send(own, blocks.at[2, :, c], 3, block_sem.at[1, i], down)

        if i > 0:
            arrived(across, other_sem.at[i])
        send(across, blocks.at[2 + 2 * parity, :, c], 6, block_sem.at[1 + parity, PEERS + i], far)
        send(across, blocks.at[0, :, c], 5, block_sem.at[0, PEERS + i], home)
        if i == 0:
            arrived(blocks.at[0, :, c], block_sem.at[0, 0])
        share(0, c, i)

    def lift(i):
        @pl.when(rises(i, up_below))
        def _():
            arrived(stash.at[:, i], stash_sem.at[i])
            send(stash.at[:, i], blocks.at[4, :, place(i, mine)], 4, block_sem.at[2, i], up)

    first, second = 2 - parity, 1 + parity

    def relay(i):
        c, d = place(i, mine), place(i, theirs)
        arrived(blocks.at[2 * first, :, d], block_sem.at[first, PEERS + i])

        @pl.when((parity == 0) | (rank(i) >= spared_next))
        def _():
            send(blocks.at[2 * first, :, d], blocks.at[2 * second, :, d], 4, block_sem.at[second, PEERS + i], onward)

        share(first, d, i)
        arrived(blocks.at[0, :, d], block_sem.at[0, PEERS + i])
        share(0, d, i)

        @pl.when(jnp.logical_not(rises(i, up_next)))
        def _():
            arrived(blocks.at[2, :, c], block_sem.at[1, i])

            @pl.when(rank(i) >= spared_next)
            def _():
                send(blocks.at[2, :, c], blocks.at[4, :, c], 4, block_sem.at[2, i], down)

            share(1, c, i)

    def raised(i):
        c = place(i, mine)

        @pl.when(rises(i, up_after))
        def _():
            arrived(blocks.at[4, :, c], block_sem.at[2, i])
            send(blocks.at[4, :, c], blocks.at[2, :, c], 4, block_sem.at[1, i], up)
            share(2, c, i)

    gain_copy.wait()
    for j in range(SIDE):
        target = wrap(x - j)
        raw_copies[j].wait()
        octet = raw.at[j].reshape(2 * ROWS * pitch, LANES)
        gain_re, gain_im = gain[0, :, :OCTET], gain[1, :, :OCTET]
        for o in range(1, SIDE):
            gain_re = jnp.where(target == o, gain[0, :, o * OCTET : (o + 1) * OCTET], gain_re)
            gain_im = jnp.where(target == o, gain[1, :, o * OCTET : (o + 1) * OCTET], gain_im)
        for s in range(OCTET):
            g_re = jnp.broadcast_to(gain_re[:, s : s + 1], (ROWS, LANES))
            g_im = jnp.broadcast_to(gain_im[:, s : s + 1], (ROWS, LANES))
            f = target * OCTET + s
            for t in range(lane_tiles):
                start = t * OCTET + s
                v_re = octet[pl.ds(start, ROWS, stride=pitch), :].astype(jnp.float32)
                v_im = octet[pl.ds(ROWS * pitch + start, ROWS, stride=pitch), :].astype(jnp.float32)
                cal[f, 0, :, t * LANES : (t + 1) * LANES] = (g_re * v_re - g_im * v_im).astype(jnp.bfloat16)
                cal[f, 1, :, t * LANES : (t + 1) * LANES] = (g_re * v_im + g_im * v_re).astype(jnp.bfloat16)

        if j == 0:
            pl.semaphore_wait(barrier, PEERS + 4)
            pltpu.make_async_copy(cal.at[me_c], blocks.at[0, :, me_c], block_sem.at[0, 0]).start()

        for k in range(1 if j == 0 else 0, SIDE):
            i = j * SIDE + k
            c = 8 * target + wrap(y - k)
            send(cal.at[c + mine], blocks.at[0, :, me_c], 0, block_sem.at[0, i], (c + mine, ablk))
            send(cal.at[c + theirs], other.at[:, i], 1, other_sem.at[i], (c + mine, ablk))
        if j < EARLY:
            direct(j)

    for i in range(EARLY, PEERS + 2 * DELAY):
        if i < PEERS:
            direct(i)
        if 0 <= i - DELAY < PEERS:
            lift(i - DELAY)
            relay(i - DELAY)
        if i >= 2 * DELAY:
            raised(i - 2 * DELAY)

    def twin(q, side):
        ref = blocks.at[2 * q + 1, :, pl.ds(0, PEERS)]
        arrived(ref, twin_sem.at[q, side])

    def diagonal_part(part):
        columns = slice(part * size // 2, (part + 1) * size // 2)
        right = blocks[0, :, part * PEERS : (part + 1) * PEERS].reshape(2, size // 2, -1)
        diagonal[0, :, columns], diagonal[1, :, columns] = product(blocks[0].reshape(2, size, -1), right, scale)

    def slot_part(k):
        right = [blocks[k, :, pl.ds(xs[o], 8)].reshape(2, LANES, -1) for o in range(2)]
        made = product(blocks[0].reshape(2, size, -1), jnp.concatenate(right, axis=1), scale)
        for o in range(2):
            for part in range(2):
                begun[k - 1, o, part] = made[part][:, o * LANES : (o + 1) * LANES]

    for i in range(PEERS):
        c, d = place(i, mine), place(i, theirs)

        @pl.when((parity == 0) | (rank(i) >= spared_after))
        def _():
            arrived(blocks.at[2 * second, :, d], block_sem.at[second, PEERS + i])
            share(second, d, i)

        @pl.when(rises(i, up_next))
        def _():
            arrived(blocks.at[2, :, c], block_sem.at[1, i])
            share(1, c, i)

        @pl.when(jnp.logical_not(rises(i, up_after)) & (rank(i) >= spared_after))
        def _():
            arrived(blocks.at[4, :, c], block_sem.at[2, i])
            share(2, c, i)

    diagonal_part(0)
    diagonal_part(1)
    twin(0, 0)
    twin(1, 0)
    slot_part(2)
    slot_part(1)
    slot_part(3)

    def sent(kind, count):
        ref = blocks.at[0, :, pl.ds(0, count)]
        pltpu.make_async_copy(ref, ref, send_sem.at[kind]).wait()

    for kind, count in ((0, 15), (1, 15), (3, 16), (5, 16), (6, 16)):
        sent(kind, count)
    count = up_below + up_after + (PEERS - parity * spared_next)
    for i in range(PEERS):
        count = count + jnp.where(rises(i, up_next) | (rank(i) < spared_next), 0, 1)
    for bit in (1, 2, 4, 8, 16, 32):

        @pl.when(lax.rem(count // bit, 2) == 1)
        def _(bit=bit):
            sent(4, bit)

    pair = blocks.at[pl.ds(0, 2)]
    pltpu.make_async_copy(pair, pair, send_sem.at[2]).wait()
    twin(0, 1)
    twin(1, 1)


def product(left, right, scale):
    def dot(a, b):
        return lax.dot_general(a, b, (((1,), (1,)), ((), ())), preferred_element_type=jnp.float32)

    real = dot(left[0], right[0]) + dot(left[1], right[1])
    imag = dot(left[1], right[0]) - dot(left[0], right[1])
    return real * scale, imag * scale


def pairs_kernel(blocks, diagonal, begun, out, made, last, sem, *, scale):
    chan, ablk = lax.axis_index("chan"), lax.axis_index("ablk")
    size = diagonal.shape[1]
    half = size // 2

    def tile(k, o):
        return pl.ds(k * size, size), pl.ds(pl.multiple_of((chan // 8 + o) % SIDE * LANES, LANES), LANES)

    copies = []

    def put(src, *where):
        copies.append(pltpu.make_async_copy(src, out.at[:, *where], sem.at[len(copies)]))
        copies[-1].start()

    put(diagonal, pl.ds(0, size))
    for k in range(1, SIDE):
        for o in range(2):
            put(begun.at[k - 1, o], *tile(k, o))

    upper = ablk >= 4

    @pl.when(jnp.logical_not(upper))
    def _():
        last[0], last[1] = product(blocks[0, :, :half], blocks[4], scale)

    @pl.when(upper)
    def _():
        last[0], last[1] = product(blocks[4, :, half:], blocks[0], scale)

    put(last, pl.ds(SIDE * size, half))
    for k in range(1, SIDE):
        right = jnp.concatenate([blocks[k, :, tile(0, o)[1], :] for o in (2, 3)], axis=1)
        both = product(blocks[0], right, scale)
        for o in range(2):
            for part in range(2):
                made[k - 1, o, part] = both[part][:, o * LANES : (o + 1) * LANES]
            put(made.at[k - 1, o], *tile(k, 2 + o))
    for copy in copies:
        copy.wait()


def body(voltages, complex_gains):
    parts, rows, channels, samples = voltages.shape
    lane_tiles = samples // LANES
    octets = channels // OCTET
    tiles = voltages.reshape(parts, rows, octets, OCTET, lane_tiles, LANES).transpose(0, 1, 2, 4, 3, 5)
    tiles = tiles.reshape(parts * rows, octets, lane_tiles * OCTET, LANES)
    size = 32 * rows
    blocks, diagonal, begun = pl.pallas_call(
        gather_kernel,
        out_shape=(
            pltpu.VMEM((5, parts, 32, rows, samples), jnp.bfloat16),
            pltpu.VMEM((parts, size, size), jnp.float32),
            pltpu.VMEM((3, 2, parts, size, LANES), jnp.float32),
        ),
        in_specs=[pl.BlockSpec(memory_space=pltpu.HBM)] * 2,
        out_specs=(pl.BlockSpec(memory_space=pltpu.VMEM),) * 3,
        scratch_shapes=[
            pltpu.VMEM((octets, parts * rows, lane_tiles * OCTET + 8, LANES), jnp.int32),
            pltpu.VMEM((parts, rows, channels), jnp.float32),
            pltpu.VMEM((channels, parts, rows, samples), jnp.bfloat16),
            pltpu.VMEM((parts, PEERS, rows, samples), jnp.bfloat16),
            pltpu.VMEM((parts, PEERS, rows, samples), jnp.bfloat16),
            pltpu.SemaphoreType.DMA((SIDE,)),
            pltpu.SemaphoreType.DMA,
            pltpu.SemaphoreType.DMA((3, 2 * PEERS)),
            pltpu.SemaphoreType.DMA((PEERS,)),
            pltpu.SemaphoreType.DMA((PEERS,)),
            pltpu.SemaphoreType.DMA((2, 2)),
            pltpu.SemaphoreType.DMA((7,)),
        ],
        compiler_params=pltpu.CompilerParams(
            collective_id=0, has_side_effects=True, vmem_limit_bytes=40 * 1024 * 1024
        ),
        name="gather",
    )(*(pltpu.with_memory_space_constraint(a, pltpu.HBM) for a in (tiles, complex_gains)))

    out = pl.pallas_call(
        functools.partial(pairs_kernel, scale=1.0 / (4.0 * samples)),
        out_shape=jax.ShapeDtypeStruct((parts, 4 * size + size // 2, size), jnp.float32),
        in_specs=[pl.BlockSpec(memory_space=pltpu.VMEM)] * 3,
        out_specs=pl.BlockSpec(memory_space=pl.ANY),
        scratch_shapes=[
            pltpu.VMEM((3, 2, parts, size, LANES), jnp.float32),
            pltpu.VMEM((parts, size // 2, size), jnp.float32),
            pltpu.SemaphoreType.DMA((14,)),
        ],
        compiler_params=pltpu.CompilerParams(vmem_limit_bytes=40 * 1024 * 1024),
        name="pairs",
    )(blocks.reshape(5, parts, size, samples), diagonal, begun)
    return out[None]


def solution(mesh):
    in_specs = (P(None, ("chan", "ablk"), None, None), P(None, ("chan", "ablk"), None))
    out_specs = P("chan", None, "ablk", None)
    return jax.shard_map(body, mesh=mesh, in_specs=in_specs, out_specs=out_specs, check_vma=False)
```

time: 200 us -> 75.5 us (0.38)
  the two profiles are of different devices: /device:TPU:1 before, /device:TPU:6 now
where the time goes in v3:
time: 75.5 us; the launch traced here: 75.4 us
  Pallas kernels  75.4 us (100%)
    pallas_call x1, Pallas kernels, body(): pl.pallas_call(gather_kernel, out_shape=(pltpu.VMEM((5, parts, 32, rows,...  71.2 us
    pallas_call x1, Pallas kernels, body(): pl.pallas_call(functools.partial(pairs_kernel, scale=1.0 / (4.0 * samples...  4.21 us

profile of v3, /device:TPU:6, one launch (start us, length us, event | category | flops | bytes accessed | tf_op | source)
XLA Modules:
  0.0 75.4 jit_solution(1403376947425929291)
XLA Ops:
  0.0 71.2 %gather.1 = (bf16[5,2,32,16,512]{4,3,2,1,0:T(8,128)(2,1)S(1)}, f32[2,512,512]{2,1,0:T(8,128)S(1)}, f32[3,2,2,512,128]{4,3,2,1,0:T(8,128)S(1)}) custom-call(s32[32,4,32,128]{3,2,1,0:T(8,128)} %bitcast.8, f32[2,16,32]{2,1,0:T(8,128)} %gain_hbm.1), custom_call_target="tpu_custom_call" | custom-call | tf_op jit(solution)/shard_map/gather/pallas_call | solution.py:333
  71.2 4.2 %pairs.1 = f32[2,2304,512]{2,1,0:T(8,128)} custom-call(bf16[5,2,512,512]{3,2,1,0:T(8,128)(2,1)S(1)} %bitcast.7, f32[2,512,512]{2,1,0:T(8,128)S(1)} %get-tuple-element.9.diagonal, f32[3,2,2,512,128]{4,3,2,1,0:T(8,128)S(1)} %get-tuple-element.10.begun), custom_call_target="tpu_custom_call" | custom-call | tf_op jit(solution)/shard_map/pairs/pallas_call | solution.py:362

commit v4 on v3

--- a/solution.py
+++ b/solution.py
@@ -16,7 +16,7 @@
 OCTET = 8
 GROUPS = 4
 UPS = 4, 4, 6, 4
-DELAY = 8
+DELAY = 10
 EARLY = 4
 
 
@@ -26,7 +26,7 @@
 
 def gather_kernel(
     volt, gain_hbm, blocks, diagonal, begun, raw, gain, cal, other, stash,
-    raw_sem, gain_sem, block_sem, other_sem, stash_sem, twin_sem, send_sem,
+    raw_sem, gain_sem, block_sem, other_sem, stash_sem, twin_sem, send_sem, column_sem,
 ):
     chan, ablk = lax.axis_index("chan"), lax.axis_index("ablk")
     x, y, parity = chan // 8, lax.rem(chan, 4), lax.rem(chan // 4, 2)
@@ -73,6 +73,11 @@
     home = flip_c, ablk
     far, onward, far_source = along(3 * parity - 1, True), along(1 - 2 * parity), along(3 * parity - 2, True)
 
+    barrier = pltpu.get_barrier_semaphore()
+    row = [(place(i, mine), ablk) for i in range(SIDE, PEERS, SIDE)]
+    for to in [up, down, home, far_source, twin_device] + [(place(i, mine), ablk) for i in range(1, SIDE)] + row:
+        pl.semaphore_signal(barrier, inc=1, device_id=to, device_id_type=MESH)
+
     gain_copy = pltpu.make_async_copy(gain_hbm, gain, gain_sem)
     gain_copy.start()
     raw_copies = []
@@ -80,11 +85,6 @@
         target = wrap(x - j)
         raw_copies.append(pltpu.make_async_copy(volt.at[:, target], raw.at[j, :, pl.ds(0, step)], raw_sem.at[j]))
         raw_copies[-1].start()
-
-    barrier = pltpu.get_barrier_semaphore()
-
-    for to in [(place(i, mine), ablk) for i in range(1, PEERS)] + [up, down, home, far_source, twin_device]:
-        pl.semaphore_signal(barrier, inc=1, device_id=to, device_id_type=MESH)
 
     def send(src, dst, kind, sem, to):
         pltpu.make_async_remote_copy(
@@ -190,8 +190,13 @@
                 cal[f, 1, :, t * LANES : (t + 1) * LANES] = (g_re * v_im + g_im * v_re).astype(jnp.bfloat16)
 
         if j == 0:
-            pl.semaphore_wait(barrier, PEERS + 4)
+            pl.semaphore_wait(barrier, 2 * (SIDE - 1) + 5)
+            for to in row:
+                pl.semaphore_signal(column_sem, inc=1, device_id=to, device_id_type=MESH)
             pltpu.make_async_copy(cal.at[me_c], blocks.at[0, :, me_c], block_sem.at[0, 0]).start()
+
+        if j == 1:
+            pl.semaphore_wait(column_sem, SIDE - 1)
 
         for k in range(1 if j == 0 else 0, SIDE):
             i = j * SIDE + k
@@ -244,8 +249,9 @@
             arrived(blocks.at[4, :, c], block_sem.at[2, i])
             share(2, c, i)
 
-    diagonal_part(0)
-    diagonal_part(1)
+        if i in (0, 3):
+            diagonal_part(i // 3)
+
     twin(0, 0)
     twin(1, 0)
     slot_part(2)
@@ -352,6 +358,7 @@
             pltpu.SemaphoreType.DMA((PEERS,)),
             pltpu.SemaphoreType.DMA((2, 2)),
             pltpu.SemaphoreType.DMA((7,)),
+            pltpu.SemaphoreType.REGULAR,
         ],
         compiler_params=pltpu.CompilerParams(
             collective_id=0, has_side_effects=True, vmem_limit_bytes=40 * 1024 * 1024

time: 75.5 us -> 73.6 us (0.975)
  the two profiles are of different devices: /device:TPU:6 before, /device:TPU:1 now
where the time goes in v4:
time: 73.6 us; the launch traced here: 72.3 us
  Pallas kernels  72.3 us (98%)
    pallas_call x1, Pallas kernels, body(): pl.pallas_call(gather_kernel, out_shape=(pltpu.VMEM((5, parts, 32, rows,...  68.1 us
    pallas_call x1, Pallas kernels, body(): pl.pallas_call(functools.partial(pairs_kernel, scale=1.0 / (4.0 * samples...  4.21 us

profile of v4, /device:TPU:1, one launch (start us, length us, event | category | flops | bytes accessed | tf_op | source)
XLA Modules:
  0.0 72.3 jit_solution(5799935501606329447)
XLA Ops:
  0.0 68.1 %gather.1 = (bf16[5,2,32,16,512]{4,3,2,1,0:T(8,128)(2,1)S(1)}, f32[2,512,512]{2,1,0:T(8,128)S(1)}, f32[3,2,2,512,128]{4,3,2,1,0:T(8,128)S(1)}) custom-call(s32[32,4,32,128]{3,2,1,0:T(8,128)} %bitcast.8, f32[2,16,32]{2,1,0:T(8,128)} %gain_hbm.1), custom_call_target="tpu_custom_call" | custom-call | tf_op jit(solution)/shard_map/gather/pallas_call | solution.py:339
  68.1 4.2 %pairs.1 = f32[2,2304,512]{2,1,0:T(8,128)} custom-call(bf16[5,2,512,512]{3,2,1,0:T(8,128)(2,1)S(1)} %bitcast.7, f32[2,512,512]{2,1,0:T(8,128)S(1)} %get-tuple-element.9.diagonal, f32[3,2,2,512,128]{4,3,2,1,0:T(8,128)S(1)} %get-tuple-element.10.begun), custom_call_target="tpu_custom_call" | custom-call | tf_op jit(solution)/shard_map/pairs/pallas_call | solution.py:369

commit v5 on v4

--- a/solution.py
+++ b/solution.py
@@ -251,10 +251,11 @@
 
         if i in (0, 3):
             diagonal_part(i // 3)
+        elif i == 8:
+            slot_part(2)
 
     twin(0, 0)
     twin(1, 0)
-    slot_part(2)
     slot_part(1)
     slot_part(3)
 

time: 73.6 us -> 73.1 us (level)
  no operation moved by 1% of the time
where the time goes in v5:
time: 73.1 us; the launch traced here: 71.7 us
  Pallas kernels  71.7 us (98%)
    pallas_call x1, Pallas kernels, body(): pl.pallas_call(gather_kernel, out_shape=(pltpu.VMEM((5, parts, 32, rows,...  67.5 us
    pallas_call x1, Pallas kernels, body(): pl.pallas_call(functools.partial(pairs_kernel, scale=1.0 / (4.0 * samples...  4.21 us

profile of v5, /device:TPU:1, one launch (start us, length us, event | category | flops | bytes accessed | tf_op | source)
XLA Modules:
  0.0 71.7 jit_solution(13632908555539954770)
XLA Ops:
  0.0 67.5 %gather.1 = (bf16[5,2,32,16,512]{4,3,2,1,0:T(8,128)(2,1)S(1)}, f32[2,512,512]{2,1,0:T(8,128)S(1)}, f32[3,2,2,512,128]{4,3,2,1,0:T(8,128)S(1)}) custom-call(s32[32,4,32,128]{3,2,1,0:T(8,128)} %bitcast.8, f32[2,16,32]{2,1,0:T(8,128)} %gain_hbm.1), custom_call_target="tpu_custom_call" | custom-call | tf_op jit(solution)/shard_map/gather/pallas_call | solution.py:340
  67.5 4.2 %pairs.1 = f32[2,2304,512]{2,1,0:T(8,128)} custom-call(bf16[5,2,512,512]{3,2,1,0:T(8,128)(2,1)S(1)} %bitcast.7, f32[2,512,512]{2,1,0:T(8,128)S(1)} %get-tuple-element.9.diagonal, f32[3,2,2,512,128]{4,3,2,1,0:T(8,128)S(1)} %get-tuple-element.10.begun), custom_call_target="tpu_custom_call" | custom-call | tf_op jit(solution)/shard_map/pairs/pallas_call | solution.py:370
